TPU v7x, 256 devices: a whole 4x4x8 slice. The times are simulated.
256 devices in a mesh: row: 32 (over z, y_lo, core), col: 4 (over x), rep: 2 (over y_hi).
Axes of the slice: x: 4, y: 4 (y_hi: 2, y_lo: 2; y = y_hi * 2 + y_lo), z: 8, core: 2. Of those that a mesh axis runs over, the one named last changes fastest.
Arguments:
- tracers: bfloat16 [16, 8388608], P('col', ('row', 'rep')), may hold values from -6 to 6
- winds: float32 [2, 8388608], P(None, ('row', 'rep')), may hold values from -6 to 6
- tile_owner: int32 [65536], P(('row', 'rep')), may hold values from 0 to 65535, as said below
- departure: int32 [65536, 3], P(('row', 'rep')), may hold values from 0 to 65535, as said below
Outputs:
- advected: bfloat16 [16, 8388608], P('col', ('row', 'rep'))
Inputs may be any that keep to these rules, and one draw needn't show every extreme that they name: `tile_owner`: A permutation of the blocks; the tiles of each device along row+rep (in that order, 1024 a device) name exactly 16 blocks of every such device. Each departure block lies within 256 blocks of its own block, counted cyclically over the 65536 blocks; that distance is reached.
All inputs are finite; a program needn't handle non-finite values.
Results may differ from a plain program's by a relative error of at most 0.0048.
Values may be sent and summed in bfloat16 or wider, within the bound.
A program may use at most 64 MiB of HBM per device.

v0:
```python
import functools

import jax
import jax.numpy as jnp
from jax import lax
from jax.experimental import pallas as pl
from jax.experimental.pallas import tpu as pltpu
from jax.sharding import PartitionSpec as P

f32, i32, bf16 = jnp.float32, jnp.int32, jnp.bfloat16
AXES = ("row", "rep")
MESH = pl.DeviceIdType.MESH
ROWS = 17
UNIT = 4096
STEP = 64


def iota(shape, dim):
    return lax.broadcasted_iota(i32, shape, dim)


def pick(cond):
    return jnp.where(cond, 1.0, 0.0).astype(bf16)


def bytes_of(code):
    return (code >> 8).astype(f32).astype(bf16), (code & 255).astype(f32).astype(bf16)


def joined(parts):
    y = (parts[:, 0:128] * 256.0 + parts[:, 128:256]).astype(i32)
    x = (parts[:, 256:384] * 256.0 + parts[:, 384:512]).astype(i32)
    return (y << 16) | (x & 65535)


def place_of(piece):
    return {"row": piece // 2, "rep": piece % 2}


def exchange(
    winds, owner, tracers, words, low, high,
    parts, snd, rcv, where, counts, send_sem, recv_sem, halo_send, halo_recv,
):
    pieces = snd.shape[0]
    blocks = winds.shape[0] // 2
    edge = low.shape[0]
    me = lax.axis_index(AXES)
    after = lax.rem(me + 1, pieces)
    before = lax.rem(me + pieces - 1, pieces)

    barrier = pltpu.get_barrier_semaphore()

    def greet(i, _):
        to = lax.rem(me + i, pieces)
        pl.semaphore_signal(barrier, inc=1, device_id=place_of(to), device_id_type=MESH)
        return 0

    lax.fori_loop(1, pieces, greet, 0)

    def encode(i, _):
        base = i * 64
        y = jnp.concatenate([winds[pl.ds((base + 8 * j) * 2, 8, stride=2), :] for j in range(8)], 0)
        x = jnp.concatenate([winds[pl.ds((base + 8 * j) * 2 + 1, 8, stride=2), :] for j in range(8)], 0)
        cy = jnp.round(jnp.tanh(y) * (6.0 * UNIT)).astype(i32)
        cx = jnp.round(jnp.tanh(x) * (4.0 * UNIT)).astype(i32)
        parts[pl.ds(pl.multiple_of(base, 64), 64), :] = jnp.concatenate(bytes_of(cy) + bytes_of(cx), 1)
        return 0

    lax.fori_loop(0, blocks // 64, encode, 0)

    lanes = iota((128, 128), 1)
    step = jnp.concatenate([pick(iota((128, 128), 0) < lanes), jnp.ones((128, 128), bf16)], 1)
    run = jnp.zeros((pieces, 128), f32)
    sums = jnp.zeros((pieces, 128), f32)
    first_lane = lax.rem(me, 8) * 16
    for g in range(blocks // 128):
        own = owner[g : g + 1, :]
        to = own // blocks
        slot = own - to * blocks
        mine = iota((pieces, 128), 0) == to
        hot = pick(mine)
        seen = jnp.dot(hot, step, preferred_element_type=f32)
        rank = jnp.sum(jnp.where(mine, seen[:, :128] + run, 0.0), axis=0, keepdims=True)
        rank = rank.astype(i32)
        run = run + seen[:, 128:]
        where[g : g + 1, :] = to * 16 + rank
        here = iota((128, 128), 0) == rank + first_lane
        for part, scale in ((slot >> 5, 32.0), (slot & 31, 1.0)):
            spread = jnp.where(here, part.astype(f32), 0.0).astype(bf16)
            sums = sums + scale * lax.dot_general(
                hot, spread, (((1,), (1,)), ((), ())), preferred_element_type=f32
            )
    counts[...] = sums.astype(i32)

    def order(i, _):
        base = i * 128
        hot = jnp.concatenate(
            [pick(iota((128, 128), 0) + base == where[g : g + 1, :]) for g in range(blocks // 128)], 1
        )
        word = joined(jnp.dot(hot, parts[...], preferred_element_type=f32))
        for j in range(8):
            snd[i * 8 + j, 0:16, :] = word[16 * j : 16 * j + 16]
            snd[i * 8 + j, 16:17, :] = counts[pl.ds(i * 8 + j, 1), :]
        return 0

    lax.fori_loop(0, blocks // 128, order, 0)

    pl.semaphore_wait(barrier, pieces - 1)

    def message(to, frm):
        return pltpu.make_async_remote_copy(
            src_ref=snd.at[to, pl.ds(0, ROWS)],
            dst_ref=rcv.at[frm, pl.ds(0, ROWS)],
            send_sem=send_sem.at[to],
            recv_sem=recv_sem.at[frm],
            device_id=place_of(to),
            device_id_type=MESH,
        )

    def start(i, _):
        message(lax.rem(me + i, pieces), me).start()
        return 0

    lax.fori_loop(1, pieces, start, 0)

    up = pltpu.make_async_remote_copy(
        src_ref=tracers.at[pl.ds(tracers.shape[0] - edge, edge)],
        dst_ref=low,
        send_sem=halo_send.at[0],
        recv_sem=halo_recv.at[0],
        device_id=place_of(after),
        device_id_type=MESH,
    )
    down = pltpu.make_async_remote_copy(
        src_ref=tracers.at[pl.ds(0, edge)],
        dst_ref=high,
        send_sem=halo_send.at[1],
        recv_sem=halo_recv.at[1],
        device_id=place_of(before),
        device_id_type=MESH,
    )
    up.start()
    down.start()
    rcv[me, 0:24, :] = snd[me, 0:24, :]

    def finish(i, _):
        other = lax.rem(me + i, pieces)
        copy = message(other, other)
        copy.wait_send()
        copy.wait_recv()
        return 0

    lax.fori_loop(1, pieces, finish, 0)

    for g in range(blocks // 128):
        where[g : g + 1, :] = functools.reduce(
            jnp.add, [rcv[g * 8 + s, 16:17, :] for s in range(8)]
        )

    def unpack(i, _):
        word = rcv[pl.ds(i * 4, 4), 0:16, :].reshape(64, 128)
        y, x = word >> 16, (word << 16) >> 16
        parts[pl.ds(pl.multiple_of(i * 64, 64), 64), :] = jnp.concatenate(bytes_of(y) + bytes_of(x), 1)
        return 0

    lax.fori_loop(0, blocks // 64, unpack, 0)

    def settle(i, _):
        base = i * 128
        hot = jnp.concatenate(
            [pick(iota((128, 128), 0) + base == where[g : g + 1, :]) for g in range(blocks // 128)], 1
        )
        words[pl.ds(pl.multiple_of(base, 128), 128), :] = joined(
            jnp.dot(hot, parts[...], preferred_element_type=f32)
        )
        return 0

    lax.fori_loop(0, blocks // 128, settle, 0)
    up.wait()
    down.wait()


def lagrange(t):
    a, b, c = t + 1.0, t - 1.0, t - 2.0
    tb, ac = t * b, a * c
    return tb * c * (-1.0 / 6.0), ac * b * 0.5, ac * t * (-0.5), a * tb * (1.0 / 6.0)


def rows_at(x, index):
    return jnp.take_along_axis(x, index, axis=0, mode="promise_in_bounds")


def folded(a, b, d):
    sub = iota((8, 128), 0)
    mine = (sub & d) == 0
    kept, moved = jnp.where(mine, a, b), jnp.where(mine, b, a)
    return kept + rows_at(moved, sub ^ d)


def transport(dep, words, tracers, low, high, out, spread, fact_y, fact_x, floors):
    blocks = words.shape[0]
    reach = low.shape[0] // 4
    total = blocks * lax.axis_size(AXES)
    shift = reach - lax.axis_index(AXES) * blocks + total
    cell_row = iota((8, 128), 1) >> 4
    cell_col = iota((8, 128), 1) & 15
    sub = iota((8, 128), 0)
    zero = jnp.zeros((8, 128), f32)

    def widen(ref, first):
        def one(i, _):
            x = ref[pl.ds(pl.multiple_of(i * 32, 32), 32), :].astype(f32)
            own = cell_row == sub
            y = jnp.where(own[None], jnp.broadcast_to(x[:, None, :], (32, 8, 128)), 0.0)
            spread[pl.ds(pl.multiple_of((first + i) * 256, 256), 256), :] = y.reshape(256, 128).astype(bf16)
            return 0

        lax.fori_loop(0, ref.shape[0] // 32, one, 0)

    widen(low, 0)
    widen(tracers, reach // 8)
    widen(high, (reach + blocks) // 8)

    def clear(i, _):
        at = pl.ds(pl.multiple_of(i * 512, 512), 512)
        fact_y[at, :] = jnp.zeros((512, 128), f32)
        fact_x[at, :] = jnp.zeros((512, 128), f32)
        return 0

    lax.fori_loop(0, blocks // 64, clear, 0)

    def factors(i, _):
        for u in range(4):
            g = i * 4 + u
            at = pl.ds(pl.multiple_of(g * 8, 8), 8)
            word = words[at, :]
            pos_y = (cell_row + 8) * UNIT - (word >> 16)
            pos_x = cell_col * UNIT - ((word << 16) >> 16)
            wy = lagrange((pos_y & (UNIT - 1)).astype(f32) * (1.0 / UNIT))
            wx = lagrange((pos_x & (UNIT - 1)).astype(f32) * (1.0 / UNIT))
            for p in range(4):
                fact_y[pl.ds(g * 64 + p, 8, stride=8), :] = wy[p]
                fact_x[pl.ds(g * 64 + p, 8, stride=8), :] = wx[p]
            floors[0, at, :] = pos_y >> 12
            floors[1, at, :] = pos_x >> 12
        return 0

    lax.fori_loop(0, blocks // 32, factors, 0)

    def two_blocks(first):
        prods = []
        for e in (0, 1):
            b = first + e
            lines = []
            for k in range(3):
                d = (dep[k, b] + shift) & (total - 1)
                lines.append(spread[pl.ds(pl.multiple_of(d * 32, 32), 32), :])
            uy = (sub + 1) - jnp.broadcast_to(floors[0, pl.ds(b, 1), :], (8, 128))
            ux = (sub + 1) - jnp.broadcast_to(floors[1, pl.ds(b, 1), :], (8, 128))
            at = pl.ds(pl.multiple_of(b * 8, 8), 8)
            gy = rows_at(fact_y[at, :], uy & 7)
            gx = rows_at(fact_x[at, :], ux & 7)
            near = (ux & 8) == 0
            cols = jnp.concatenate([jnp.where(near, gx, zero), jnp.where(near, zero, gx)], 0).astype(bf16)
            sums = jnp.dot(
                jnp.concatenate(lines, 0), jnp.concatenate([cols] * 8, 0), preferred_element_type=f32
            )
            in0, in1 = uy >= 0, uy >= -8
            for t in range(4):
                r0, r1, r2 = (sums[32 * k + 8 * t : 32 * k + 8 * t + 8] for k in range(3))
                prods.append(jnp.where(in0, r0, jnp.where(in1, r1, r2)) * gy)
        for d in (4, 2, 1):
            prods = [folded(prods[i], prods[i + d], d) for i in range(d)]
        return prods[0]

    def some(i, _):
        for q in range(0, STEP, 4):
            b = i * STEP + q
            four = jnp.concatenate([two_blocks(b), two_blocks(b + 2)], 0).astype(bf16)
            out[pl.ds(pl.multiple_of(b * 4, 16), 16), :] = four
        return 0

    lax.fori_loop(0, blocks // STEP, some, 0)


def in_vmem(n):
    return [pl.BlockSpec(memory_space=pltpu.VMEM)] * n


def on_device(tracers, winds, tile_owner, departure):
    pieces = lax.axis_size(AXES)
    blocks = tile_owner.shape[0]
    panel = tracers.shape[0]
    edge = blocks // 4 * panel
    lines = tracers.reshape(panel, blocks, 128).transpose(1, 0, 2).reshape(blocks * panel, 128)
    wind_lines = winds.reshape(2, blocks, 128).transpose(1, 0, 2).reshape(blocks * 2, 128)
    words, low, high = pl.pallas_call(
        exchange,
        out_shape=(
            jax.ShapeDtypeStruct((blocks, 128), i32),
            jax.ShapeDtypeStruct((edge, 128), bf16),
            jax.ShapeDtypeStruct((edge, 128), bf16),
        ),
        in_specs=in_vmem(3),
        out_specs=tuple(in_vmem(3)),
        scratch_shapes=[
            pltpu.VMEM((blocks, 512), bf16),
            pltpu.VMEM((pieces, 24, 128), i32),
            pltpu.VMEM((pieces, 24, 128), i32),
            pltpu.VMEM((8, 128), i32),
            pltpu.VMEM((pieces, 128), i32),
            pltpu.SemaphoreType.DMA((pieces,)),
            pltpu.SemaphoreType.DMA((pieces,)),
            pltpu.SemaphoreType.DMA((2,)),
            pltpu.SemaphoreType.DMA((2,)),
        ],
        compiler_params=pltpu.CompilerParams(
            collective_id=0, has_side_effects=True, vmem_limit_bytes=40 << 20
        ),
    )(wind_lines, tile_owner.reshape(blocks // 128, 128), lines)
    out = pl.pallas_call(
        transport,
        out_shape=jax.ShapeDtypeStruct((blocks * panel, 128), bf16),
        in_specs=[pl.BlockSpec(memory_space=pltpu.SMEM)] + in_vmem(4),
        out_specs=in_vmem(1)[0],
        scratch_shapes=[
            pltpu.VMEM((blocks * 48, 128), bf16),
            pltpu.VMEM((blocks * 8, 128), f32),
            pltpu.VMEM((blocks * 8, 128), f32),
            pltpu.VMEM((2, blocks, 128), i32),
        ],
        compiler_params=pltpu.CompilerParams(vmem_limit_bytes=48 << 20),
    )(departure.T, words, lines, low, high)
    return out.reshape(blocks, panel, 128).transpose(1, 0, 2).reshape(panel, blocks * 128)


def solution(mesh):
    placed = (
        P("col", AXES),
        P(None, AXES),
        P(AXES),
        P(AXES, None),
    )
    return jax.shard_map(
        on_device, mesh=mesh, in_specs=placed, out_specs=P("col", AXES), check_vma=False
    )
```

profile of v0, /device:TPU:1, one launch (start us, length us, event | category | flops | bytes accessed | tf_op | source)
XLA Modules:
  0.0 59.3 jit_solution(11617087965967540602)
XLA Ops:
  0.0 0.0 copy-start.4
  0.0 0.7 %copy-done.4 = s32[1024]{0:T(1024)S(1)} copy-done((s32[1024]{0:T(1024)S(1)}, s32[1024]{0:T(1024)}, u32[]{:S(2)}) %copy-start.4) | copy-done | bytes 4120
  0.7 0.0 copy-start
  0.7 1.2 %copy-done = bf16[4,131072]{1,0:T(4,128)(2,1)S(1)} copy-done((bf16[4,131072]{1,0:T(4,128)(2,1)S(1)}, bf16[4,131072]{1,0:T(4,128)(2,1)}, u32[]{:S(2)}) %copy-start) | copy-done | bytes 1048600
  1.9 0.0 copy-start.2
  1.9 1.2 %copy-done.2 = f32[2,131072]{1,0:T(2,128)S(1)} copy-done((f32[2,131072]{1,0:T(2,128)S(1)}, f32[2,131072]{1,0:T(2,128)}, u32[]{:S(2)}) %copy-start.2) | copy-done | bytes 1048600
  3.1 0.0 copy-start.1
  3.1 0.0 copy-start.3
  3.1 35.8 %shard_map.46 = (s32[1024,128]{1,0:T(8,128)S(1)}, bf16[1024,128]{1,0:T(8,128)(2,1)S(1)}, bf16[1024,128]{1,0:T(8,128)(2,1)S(1)}) custom-call(f32[2048,128]{1,0:T(8,128)S(1)} %bitcast.19, s32[8,128]{1,0:T(8,128)S(1)} %bitcast.21, bf16[4096,128]{1,0:T(8,128)(2,1)S(1)} %bitcast.17), custom_call_target="tpu_custom_call" | custom-call | tf_op jit(solution)/shard_map/pallas_call | solution.py:297
  39.0 0.0 copy-done.1
  39.0 0.0 copy-done.3
  39.0 20.3 %shard_map.47 = bf16[4096,128]{1,0:T(8,128)(2,1)} custom-call(s32[3,1024]{1,0:T(4,128)S(1)} %bitcast.20, s32[1024,128]{1,0:T(8,128)S(1)} %get-tuple-element.8.words, bf16[4096,128]{1,0:T(8,128)(2,1)S(1)} %bitcast.18, bf16[1024,128]{1,0:T(8,128)(2,1)S(1)} %get-tuple-element.9.low, bf16[1024,128]{1,0:T(8,128)(2,1)S(1)} %get-tuple-element.10.high), custom_call_target="tpu_custom_call" | custom-call | tf_op jit(solution)/shard_map/pallas_call | solution.py:321
Async XLA Ops:
  0.0 0.7 %copy-start.4 = (s32[1024]{0:T(1024)S(1)}, s32[1024]{0:T(1024)}, u32[]{:S(2)}) copy-start(s32[1024]{0:T(1024)} %param.6) | copy-start | bytes 12292
  0.7 1.2 %copy-start = (bf16[4,131072]{1,0:T(4,128)(2,1)S(1)}, bf16[4,131072]{1,0:T(4,128)(2,1)}, u32[]{:S(2)}) copy-start(bf16[4,131072]{1,0:T(4,128)(2,1)} %param.4) | copy-start | bytes 3145732
  1.9 1.2 %copy-start.2 = (f32[2,131072]{1,0:T(2,128)S(1)}, f32[2,131072]{1,0:T(2,128)}, u32[]{:S(2)}) copy-start(f32[2,131072]{1,0:T(2,128)} %param.5) | copy-start | bytes 3145732
  3.1 35.9 %copy-start.1 = (bf16[4,131072]{1,0:T(4,128)(2,1)S(1)}, bf16[4,131072]{1,0:T(4,128)(2,1)}, u32[]{:S(2)}) copy-start(bf16[4,131072]{1,0:T(4,128)(2,1)} %param.4) | copy-start | bytes 3145732
  3.1 35.9 %copy-start.3 = (s32[1024,3]{0,1:T(4,128)S(1)}, s32[1024,3]{0,1:T(4,128)}, u32[]{:S(2)}) copy-start(s32[1024,3]{0,1:T(4,128)} %param.7) | copy-start | bytes 36868
where the time goes:
time: 59.5 us; the launch traced here: 59.3 us
  Pallas kernels  56.2 us (94%)
  local copies, waits for them, and re-layouts  3.14 us (5%)
    pallas_call x1, Pallas kernels, on_device(): pl.pallas_call(exchange, out_shape=(jax.ShapeDtypeStruct((blocks, 128), i...  35.8 us
    pallas_call x1, Pallas kernels, on_device(): pl.pallas_call(transport, out_shape=jax.ShapeDtypeStruct((blocks * panel,...  20.3 us
    unnamed x10, local copies, waits for them, and re-layouts  3.14 us

commit v1 on v0

--- a/solution.py
+++ b/solution.py
@@ -10,7 +10,7 @@
 f32, i32, bf16 = jnp.float32, jnp.int32, jnp.bfloat16
 AXES = ("row", "rep")
 MESH = pl.DeviceIdType.MESH
-ROWS = 17
+ROWS = 5
 UNIT = 4096
 STEP = 64
 
@@ -38,13 +38,16 @@
 
 
 def exchange(
-    winds, owner, tracers, words, low, high,
-    parts, snd, rcv, where, counts, send_sem, recv_sem, halo_send, halo_recv,
+    winds_hbm, owner_hbm, tracers_hbm, words, spread,
+    winds, owner, tracers, low, high, parts, snd, rcv, every, where,
+    send_sem, recv_sem, halo_send, halo_recv, pass_send, pass_recv, load_sem,
 ):
     pieces = snd.shape[0]
-    blocks = winds.shape[0] // 2
+    blocks = words.shape[0]
     edge = low.shape[0]
+    share = blocks // 4
     me = lax.axis_index(AXES)
+    col = lax.axis_index("col")
     after = lax.rem(me + 1, pieces)
     before = lax.rem(me + pieces - 1, pieces)
 
@@ -56,23 +59,23 @@
         return 0
 
     lax.fori_loop(1, pieces, greet, 0)
-
-    def encode(i, _):
-        base = i * 64
-        y = jnp.concatenate([winds[pl.ds((base + 8 * j) * 2, 8, stride=2), :] for j in range(8)], 0)
-        x = jnp.concatenate([winds[pl.ds((base + 8 * j) * 2 + 1, 8, stride=2), :] for j in range(8)], 0)
-        cy = jnp.round(jnp.tanh(y) * (6.0 * UNIT)).astype(i32)
-        cx = jnp.round(jnp.tanh(x) * (4.0 * UNIT)).astype(i32)
-        parts[pl.ds(pl.multiple_of(base, 64), 64), :] = jnp.concatenate(bytes_of(cy) + bytes_of(cx), 1)
-        return 0
-
-    lax.fori_loop(0, blocks // 64, encode, 0)
-
+    for c in range(1, 4):
+        peer = {"col": lax.rem(col + c, 4)}
+        pl.semaphore_signal(barrier, inc=1, device_id=peer, device_id_type=MESH)
+
+    load_owner = pltpu.make_async_copy(owner_hbm, owner, load_sem.at[0])
+    load_winds = pltpu.make_async_copy(winds_hbm, winds, load_sem.at[1])
+    load_tracers = pltpu.make_async_copy(tracers_hbm, tracers, load_sem.at[2])
+    load_owner.start()
+    load_winds.start()
+    load_tracers.start()
+
+    load_owner.wait()
     lanes = iota((128, 128), 1)
     step = jnp.concatenate([pick(iota((128, 128), 0) < lanes), jnp.ones((128, 128), bf16)], 1)
     run = jnp.zeros((pieces, 128), f32)
     sums = jnp.zeros((pieces, 128), f32)
-    first_lane = lax.rem(me, 8) * 16
+    first_lane = lax.rem(me, 32) * 4
     for g in range(blocks // 128):
         own = owner[g : g + 1, :]
         to = own // blocks
@@ -81,31 +84,41 @@
         hot = pick(mine)
         seen = jnp.dot(hot, step, preferred_element_type=f32)
         rank = jnp.sum(jnp.where(mine, seen[:, :128] + run, 0.0), axis=0, keepdims=True)
-        rank = rank.astype(i32)
+        rank = rank.astype(i32) - 4 * col
         run = run + seen[:, 128:]
-        where[g : g + 1, :] = to * 16 + rank
-        here = iota((128, 128), 0) == rank + first_lane
+        here = (rank >= 0) & (rank < 4)
+        where[g : g + 1, :] = jnp.where(here, to * 4 + rank, -1)
+        lane = iota((128, 128), 0) == jnp.where(here, rank + first_lane, -1)
         for part, scale in ((slot >> 5, 32.0), (slot & 31, 1.0)):
-            spread = jnp.where(here, part.astype(f32), 0.0).astype(bf16)
+            spot = jnp.where(lane, part.astype(f32), 0.0).astype(bf16)
             sums = sums + scale * lax.dot_general(
-                hot, spread, (((1,), (1,)), ((), ())), preferred_element_type=f32
+                hot, spot, (((1,), (1,)), ((), ())), preferred_element_type=f32
             )
-    counts[...] = sums.astype(i32)
-
-    def order(i, _):
-        base = i * 128
-        hot = jnp.concatenate(
-            [pick(iota((128, 128), 0) + base == where[g : g + 1, :]) for g in range(blocks // 128)], 1
+    for d in range(pieces):
+        snd[d, 4:5, :] = sums[d : d + 1].astype(i32)
+
+    load_winds.wait()
+
+    def encode(i, _):
+        base = i * 64
+        y = jnp.concatenate([winds[pl.ds((base + 8 * j) * 2, 8, stride=2), :] for j in range(8)], 0)
+        x = jnp.concatenate([winds[pl.ds((base + 8 * j) * 2 + 1, 8, stride=2), :] for j in range(8)], 0)
+        cy = jnp.round(jnp.tanh(y) * (6.0 * UNIT)).astype(i32)
+        cx = jnp.round(jnp.tanh(x) * (4.0 * UNIT)).astype(i32)
+        parts[pl.ds(pl.multiple_of(base, 64), 64), :] = jnp.concatenate(bytes_of(cy) + bytes_of(cx), 1)
+        return 0
+
+    lax.fori_loop(0, blocks // 64, encode, 0)
+
+    def one_hot(base, height):
+        return jnp.concatenate(
+            [pick(iota((height, 128), 0) + base == where[g : g + 1, :]) for g in range(blocks // 128)], 1
         )
-        word = joined(jnp.dot(hot, parts[...], preferred_element_type=f32))
-        for j in range(8):
-            snd[i * 8 + j, 0:16, :] = word[16 * j : 16 * j + 16]
-            snd[i * 8 + j, 16:17, :] = counts[pl.ds(i * 8 + j, 1), :]
-        return 0
-
-    lax.fori_loop(0, blocks // 128, order, 0)
-
-    pl.semaphore_wait(barrier, pieces - 1)
+
+    word = joined(jnp.dot(one_hot(0, share), parts[...], preferred_element_type=f32))
+    snd[:, 0:4, :] = word.reshape(pieces, 4, 128)
+
+    pl.semaphore_wait(barrier, pieces + 2)
 
     def message(to, frm):
         return pltpu.make_async_remote_copy(
@@ -124,7 +137,7 @@
     lax.fori_loop(1, pieces, start, 0)
 
     up = pltpu.make_async_remote_copy(
-        src_ref=tracers.at[pl.ds(tracers.shape[0] - edge, edge)],
+        src_ref=tracers_hbm.at[pl.ds(tracers.shape[0] - edge, edge)],
         dst_ref=low,
         send_sem=halo_send.at[0],
         recv_sem=halo_recv.at[0],
@@ -132,7 +145,7 @@
         device_id_type=MESH,
     )
     down = pltpu.make_async_remote_copy(
-        src_ref=tracers.at[pl.ds(0, edge)],
+        src_ref=tracers_hbm.at[pl.ds(0, edge)],
         dst_ref=high,
         send_sem=halo_send.at[1],
         recv_sem=halo_recv.at[1],
@@ -141,7 +154,21 @@
     )
     up.start()
     down.start()
-    rcv[me, 0:24, :] = snd[me, 0:24, :]
+    rcv[me, 0:ROWS, :] = snd[me, 0:ROWS, :]
+
+    own_row = (iota((8, 128), 1) >> 4) == iota((8, 128), 0)
+
+    def widen(ref, first):
+        def one(i, _):
+            x = ref[pl.ds(pl.multiple_of(i * 32, 32), 32), :].astype(f32)
+            y = jnp.where(own_row[None], jnp.broadcast_to(x[:, None, :], (32, 8, 128)), 0.0)
+            spread[pl.ds(pl.multiple_of((first + i) * 256, 256), 256), :] = y.reshape(256, 128).astype(bf16)
+            return 0
+
+        lax.fori_loop(0, ref.shape[0] // 32, one, 0)
+
+    load_tracers.wait()
+    widen(tracers, edge // 32)
 
     def finish(i, _):
         other = lax.rem(me + i, pieces)
@@ -152,32 +179,49 @@
 
     lax.fori_loop(1, pieces, finish, 0)
 
-    for g in range(blocks // 128):
-        where[g : g + 1, :] = functools.reduce(
-            jnp.add, [rcv[g * 8 + s, 16:17, :] for s in range(8)]
+    every[col, 0:share, :] = rcv[:, 0:4, :].reshape(share, 128)
+    for h in range(2):
+        rows = [rcv[32 * h + s, 4:5, :] for s in range(32)]
+        every[col, share + h : share + h + 1, :] = functools.reduce(jnp.add, rows)
+
+    def handed(to, frm):
+        return pltpu.make_async_remote_copy(
+            src_ref=every.at[col],
+            dst_ref=every.at[frm],
+            send_sem=pass_send.at[to],
+            recv_sem=pass_recv.at[frm],
+            device_id={"col": to},
+            device_id_type=MESH,
         )
 
-    def unpack(i, _):
-        word = rcv[pl.ds(i * 4, 4), 0:16, :].reshape(64, 128)
-        y, x = word >> 16, (word << 16) >> 16
-        parts[pl.ds(pl.multiple_of(i * 64, 64), 64), :] = jnp.concatenate(bytes_of(y) + bytes_of(x), 1)
-        return 0
-
-    lax.fori_loop(0, blocks // 64, unpack, 0)
+    for c in range(1, 4):
+        handed(lax.rem(col + c, 4), col).start()
+    for c in range(1, 4):
+        other = lax.rem(col + c, 4)
+        copy = handed(other, other)
+        copy.wait_send()
+        copy.wait_recv()
+
+    for c in range(4):
+        where[2 * c : 2 * c + 2, :] = every[c, share : share + 2, :]
+        for i in range(4):
+            word = every[c, 64 * i : 64 * i + 64, :]
+            y, x = word >> 16, (word << 16) >> 16
+            at = c * share + 64 * i
+            parts[at : at + 64, :] = jnp.concatenate(bytes_of(y) + bytes_of(x), 1)
 
     def settle(i, _):
-        base = i * 128
-        hot = jnp.concatenate(
-            [pick(iota((128, 128), 0) + base == where[g : g + 1, :]) for g in range(blocks // 128)], 1
+        base = i * share
+        words[pl.ds(pl.multiple_of(base, share), share), :] = joined(
+            jnp.dot(one_hot(base, share), parts[...], preferred_element_type=f32)
         )
-        words[pl.ds(pl.multiple_of(base, 128), 128), :] = joined(
-            jnp.dot(hot, parts[...], preferred_element_type=f32)
-        )
-        return 0
-
-    lax.fori_loop(0, blocks // 128, settle, 0)
+        return 0
+
+    lax.fori_loop(0, 4, settle, 0)
     up.wait()
+    widen(low, 0)
     down.wait()
+    widen(high, (edge + tracers.shape[0]) // 32)
 
 
 def lagrange(t):
@@ -197,29 +241,15 @@
     return kept + rows_at(moved, sub ^ d)
 
 
-def transport(dep, words, tracers, low, high, out, spread, fact_y, fact_x, floors):
+def transport(dep, words, spread, out, fact_y, fact_x, floors):
     blocks = words.shape[0]
-    reach = low.shape[0] // 4
+    reach = blocks // 4
     total = blocks * lax.axis_size(AXES)
     shift = reach - lax.axis_index(AXES) * blocks + total
     cell_row = iota((8, 128), 1) >> 4
     cell_col = iota((8, 128), 1) & 15
     sub = iota((8, 128), 0)
     zero = jnp.zeros((8, 128), f32)
-
-    def widen(ref, first):
-        def one(i, _):
-            x = ref[pl.ds(pl.multiple_of(i * 32, 32), 32), :].astype(f32)
-            own = cell_row == sub
-            y = jnp.where(own[None], jnp.broadcast_to(x[:, None, :], (32, 8, 128)), 0.0)
-            spread[pl.ds(pl.multiple_of((first + i) * 256, 256), 256), :] = y.reshape(256, 128).astype(bf16)
-            return 0
-
-        lax.fori_loop(0, ref.shape[0] // 32, one, 0)
-
-    widen(low, 0)
-    widen(tracers, reach // 8)
-    widen(high, (reach + blocks) // 8)
 
     def clear(i, _):
         at = pl.ds(pl.multiple_of(i * 512, 512), 512)
@@ -294,43 +324,50 @@
     edge = blocks // 4 * panel
     lines = tracers.reshape(panel, blocks, 128).transpose(1, 0, 2).reshape(blocks * panel, 128)
     wind_lines = winds.reshape(2, blocks, 128).transpose(1, 0, 2).reshape(blocks * 2, 128)
-    words, low, high = pl.pallas_call(
+    dma = pltpu.SemaphoreType.DMA
+    words, spread = pl.pallas_call(
         exchange,
         out_shape=(
             jax.ShapeDtypeStruct((blocks, 128), i32),
-            jax.ShapeDtypeStruct((edge, 128), bf16),
-            jax.ShapeDtypeStruct((edge, 128), bf16),
+            jax.ShapeDtypeStruct((blocks * 48, 128), bf16),
         ),
-        in_specs=in_vmem(3),
-        out_specs=tuple(in_vmem(3)),
+        in_specs=[pl.BlockSpec(memory_space=pltpu.HBM)] * 3,
+        out_specs=tuple(in_vmem(2)),
         scratch_shapes=[
+            pltpu.VMEM((blocks * 2, 128), f32),
+            pltpu.VMEM((blocks // 128, 128), i32),
+            pltpu.VMEM((blocks * panel, 128), bf16),
+            pltpu.VMEM((edge, 128), bf16),
+            pltpu.VMEM((edge, 128), bf16),
             pltpu.VMEM((blocks, 512), bf16),
-            pltpu.VMEM((pieces, 24, 128), i32),
-            pltpu.VMEM((pieces, 24, 128), i32),
+            pltpu.VMEM((pieces, 8, 128), i32),
+            pltpu.VMEM((pieces, 8, 128), i32),
+            pltpu.VMEM((4, blocks // 4 + 8, 128), i32),
             pltpu.VMEM((8, 128), i32),
-            pltpu.VMEM((pieces, 128), i32),
-            pltpu.SemaphoreType.DMA((pieces,)),
-            pltpu.SemaphoreType.DMA((pieces,)),
-            pltpu.SemaphoreType.DMA((2,)),
-            pltpu.SemaphoreType.DMA((2,)),
+            dma((pieces,)),
+            dma((pieces,)),
+            dma((2,)),
+            dma((2,)),
+            dma((4,)),
+            dma((4,)),
+            dma((3,)),
         ],
         compiler_params=pltpu.CompilerParams(
-            collective_id=0, has_side_effects=True, vmem_limit_bytes=40 << 20
+            collective_id=0, has_side_effects=True, vmem_limit_bytes=36 << 20
         ),
     )(wind_lines, tile_owner.reshape(blocks // 128, 128), lines)
     out = pl.pallas_call(
         transport,
         out_shape=jax.ShapeDtypeStruct((blocks * panel, 128), bf16),
-        in_specs=[pl.BlockSpec(memory_space=pltpu.SMEM)] + in_vmem(4),
+        in_specs=[pl.BlockSpec(memory_space=pltpu.SMEM)] + in_vmem(2),
         out_specs=in_vmem(1)[0],
         scratch_shapes=[
-            pltpu.VMEM((blocks * 48, 128), bf16),
             pltpu.VMEM((blocks * 8, 128), f32),
             pltpu.VMEM((blocks * 8, 128), f32),
             pltpu.VMEM((2, blocks, 128), i32),
         ],
-        compiler_params=pltpu.CompilerParams(vmem_limit_bytes=48 << 20),
-    )(departure.T, words, lines, low, high)
+        compiler_params=pltpu.CompilerParams(vmem_limit_bytes=36 << 20),
+    )(departure.T, words, spread)
     return out.reshape(blocks, panel, 128).transpose(1, 0, 2).reshape(panel, blocks * 128)
 
 

time: 59.5 us -> 55.6 us (0.934)
  Pallas kernels: 56.2 us -> 51.5 us
  local copies, waits for them, and re-layouts: 3.14 us -> 3.85 us
    pallas_call x1, Pallas kernels: 20.3 us -> 15.4 us  [on_device(): pl.pallas_call(transport, out_shape=jax.ShapeDtypeStruct((blocks * panel,...]
    unnamed x10 -> x8, local copies, waits for them, and re-layouts: 3.14 us -> 3.85 us
where the time goes in v1:
time: 55.6 us; the launch traced here: 55.3 us
  Pallas kernels  51.5 us (93%)
  local copies, waits for them, and re-layouts  3.85 us (7%)
    pallas_call x1, Pallas kernels, on_device(): pl.pallas_call(exchange, out_shape=(jax.ShapeDtypeStruct((blocks, 128), i...  36.1 us
    pallas_call x1, Pallas kernels, on_device(): pl.pallas_call(transport, out_shape=jax.ShapeDtypeStruct((blocks * panel,...  15.4 us
    unnamed x8, local copies, waits for them, and re-layouts  3.85 us

profile of v1, /device:TPU:1, one launch (start us, length us, event | category | flops | bytes accessed | tf_op | source)
XLA Modules:
  0.0 55.3 jit_solution(10155508731377509814)
XLA Ops:
  0.0 0.0 copy-start
  0.0 1.2 %copy-done = f32[2,131072]{1,0:T(2,128)S(1)} copy-done((f32[2,131072]{1,0:T(2,128)S(1)}, f32[2,131072]{1,0:T(2,128)}, u32[]{:S(2)}) %copy-start) | copy-done | bytes 1048600
  1.2 0.0 copy-start.1
  1.2 1.2 %copy-done.1 = bf16[4,131072]{1,0:T(4,128)(2,1)S(1)} copy-done((bf16[4,131072]{1,0:T(4,128)(2,1)S(1)}, bf16[4,131072]{1,0:T(4,128)(2,1)}, u32[]{:S(2)}) %copy-start.1) | copy-done | bytes 1048600
  2.5 0.0 copy-start.3
  2.5 0.7 %copy-done.3 = s32[1024]{0:T(1024)S(1)} copy-done((s32[1024]{0:T(1024)S(1)}, s32[1024]{0:T(1024)}, u32[]{:S(2)}) %copy-start.3) | copy-done | bytes 4120
  3.1 36.1 %shard_map.46 = (s32[1024,128]{1,0:T(8,128)S(1)}, bf16[49152,128]{1,0:T(8,128)(2,1)S(1)}) custom-call(f32[2048,128]{1,0:T(8,128)S(1)} %bitcast.17, s32[8,128]{1,0:T(8,128)S(1)} %bitcast.20, bf16[4096,128]{1,0:T(8,128)(2,1)S(1)} %bitcast.18), custom_call_target="tpu_custom_call" | custom-call | tf_op jit(solution)/shard_map/pallas_call | solution.py:328
  39.2 0.0 copy-start.2
  39.2 0.7 %copy-done.2 = s32[1024,3]{0,1:T(4,128)S(1)} copy-done((s32[1024,3]{0,1:T(4,128)S(1)}, s32[1024,3]{0,1:T(4,128)}, u32[]{:S(2)}) %copy-start.2) | copy-done | bytes 12312
  40.0 15.4 %shard_map.47 = bf16[4096,128]{1,0:T(8,128)(2,1)} custom-call(s32[3,1024]{1,0:T(4,128)S(1)} %bitcast.19, s32[1024,128]{1,0:T(8,128)S(1)} %get-tuple-element.7.words, bf16[49152,128]{1,0:T(8,128)(2,1)S(1)} %get-tuple-element.8.spread), custom_call_target="tpu_custom_call" | custom-call | tf_op jit(solution)/shard_map/pallas_call | solution.py:359
Async XLA Ops:
  0.0 1.2 %copy-start = (f32[2,131072]{1,0:T(2,128)S(1)}, f32[2,131072]{1,0:T(2,128)}, u32[]{:S(2)}) copy-start(f32[2,131072]{1,0:T(2,128)} %param.5) | copy-start | bytes 3145732
  1.2 1.2 %copy-start.1 = (bf16[4,131072]{1,0:T(4,128)(2,1)S(1)}, bf16[4,131072]{1,0:T(4,128)(2,1)}, u32[]{:S(2)}) copy-start(bf16[4,131072]{1,0:T(4,128)(2,1)} %param.4) | copy-start | bytes 3145732
  2.5 0.7 %copy-start.3 = (s32[1024]{0:T(1024)S(1)}, s32[1024]{0:T(1024)}, u32[]{:S(2)}) copy-start(s32[1024]{0:T(1024)} %param.6) | copy-start | bytes 12292
  39.2 0.7 %copy-start.2 = (s32[1024,3]{0,1:T(4,128)S(1)}, s32[1024,3]{0,1:T(4,128)}, u32[]{:S(2)}) copy-start(s32[1024,3]{0,1:T(4,128)} %param.7) | copy-start | bytes 36868

commit v2 on v1

--- a/solution.py
+++ b/solution.py
@@ -37,9 +37,10 @@
     return {"row": piece // 2, "rep": piece % 2}
 
 
-def exchange(
-    winds_hbm, owner_hbm, tracers_hbm, words, spread,
-    winds, owner, tracers, low, high, parts, snd, rcv, every, where,
+def advect(
+    winds_hbm, owner_hbm, tracers_hbm, dep_hbm, out,
+    winds, owner, tracers, dep, low, high, parts, snd, rcv, every, where,
+    words, spread, fact_y, fact_x, floors,
     send_sem, recv_sem, halo_send, halo_recv, pass_send, pass_recv, load_sem,
 ):
     pieces = snd.shape[0]
@@ -59,9 +60,9 @@
         return 0
 
     lax.fori_loop(1, pieces, greet, 0)
-    for c in range(1, 4):
-        peer = {"col": lax.rem(col + c, 4)}
-        pl.semaphore_signal(barrier, inc=1, device_id=peer, device_id_type=MESH)
+    left, right = lax.rem(col + 3, 4), lax.rem(col + 1, 4)
+    for c in (left, right):
+        pl.semaphore_signal(barrier, inc=1, device_id={"col": c}, device_id_type=MESH)
 
     load_owner = pltpu.make_async_copy(owner_hbm, owner, load_sem.at[0])
     load_winds = pltpu.make_async_copy(winds_hbm, winds, load_sem.at[1])
@@ -69,6 +70,8 @@
     load_owner.start()
     load_winds.start()
     load_tracers.start()
+    load_dep = pltpu.make_async_copy(dep_hbm, dep, load_sem.at[3])
+    load_dep.start()
 
     load_owner.wait()
     lanes = iota((128, 128), 1)
@@ -118,7 +121,7 @@
     word = joined(jnp.dot(one_hot(0, share), parts[...], preferred_element_type=f32))
     snd[:, 0:4, :] = word.reshape(pieces, 4, 128)
 
-    pl.semaphore_wait(barrier, pieces + 2)
+    pl.semaphore_wait(barrier, pieces + 1)
 
     def message(to, frm):
         return pltpu.make_async_remote_copy(
@@ -152,8 +155,6 @@
         device_id=place_of(before),
         device_id_type=MESH,
     )
-    up.start()
-    down.start()
     rcv[me, 0:ROWS, :] = snd[me, 0:ROWS, :]
 
     own_row = (iota((8, 128), 1) >> 4) == iota((8, 128), 0)
@@ -162,13 +163,14 @@
         def one(i, _):
             x = ref[pl.ds(pl.multiple_of(i * 32, 32), 32), :].astype(f32)
             y = jnp.where(own_row[None], jnp.broadcast_to(x[:, None, :], (32, 8, 128)), 0.0)
-            spread[pl.ds(pl.multiple_of((first + i) * 256, 256), 256), :] = y.reshape(256, 128).astype(bf16)
+            spread[pl.ds((first + i) * 8, 8)] = y.reshape(8, 32, 128).astype(bf16)
             return 0
 
         lax.fori_loop(0, ref.shape[0] // 32, one, 0)
 
     load_tracers.wait()
     widen(tracers, edge // 32)
+    clear_factors(fact_y, fact_x)
 
     def finish(i, _):
         other = lax.rem(me + i, pieces)
@@ -184,23 +186,42 @@
         rows = [rcv[32 * h + s, 4:5, :] for s in range(32)]
         every[col, share + h : share + h + 1, :] = functools.reduce(jnp.add, rows)
 
-    def handed(to, frm):
+    cut = (share + 8) // 16 * 8 + 8
+
+    def handed(origin, half, to, send):
+        at = pl.ds(0, cut) if half == 0 else pl.ds(cut, share + 8 - cut)
         return pltpu.make_async_remote_copy(
-            src_ref=every.at[col],
-            dst_ref=every.at[frm],
-            send_sem=pass_send.at[to],
-            recv_sem=pass_recv.at[frm],
+            src_ref=every.at[origin, at],
+            dst_ref=every.at[origin, at],
+            send_sem=pass_send.at[send],
+            recv_sem=pass_recv.at[origin, half],
             device_id={"col": to},
             device_id_type=MESH,
         )
 
-    for c in range(1, 4):
-        handed(lax.rem(col + c, 4), col).start()
-    for c in range(1, 4):
-        other = lax.rem(col + c, 4)
-        copy = handed(other, other)
+    far = lax.rem(col + 2, 4)
+    sends = [
+        handed(col, 0, right, 0),
+        handed(col, 1, left, 1),
+        handed(col, 1, right, 2),
+        handed(col, 0, left, 3),
+    ]
+    for copy in sends:
+        copy.start()
+    up.start()
+    down.start()
+    handed(left, 0, left, 0).wait_recv()
+    sends.append(handed(left, 0, right, 4))
+    sends[-1].start()
+    handed(right, 1, right, 0).wait_recv()
+    sends.append(handed(right, 1, left, 5))
+    sends[-1].start()
+    handed(left, 1, left, 0).wait_recv()
+    handed(right, 0, right, 0).wait_recv()
+    handed(far, 0, left, 0).wait_recv()
+    handed(far, 1, right, 0).wait_recv()
+    for copy in sends:
         copy.wait_send()
-        copy.wait_recv()
 
     for c in range(4):
         where[2 * c : 2 * c + 2, :] = every[c, share : share + 2, :]
@@ -218,10 +239,31 @@
         return 0
 
     lax.fori_loop(0, 4, settle, 0)
+    load_dep.wait()
+    step_of = transport(dep, words, spread, out, fact_y, fact_x, floors)
+    steps = blocks // STEP
+    side = steps // 4
+
+    lax.fori_loop(side, steps - side, step_of, 0)
     up.wait()
     widen(low, 0)
     down.wait()
     widen(high, (edge + tracers.shape[0]) // 32)
+
+    def outer(i, _):
+        return step_of(i + (i // side) * (steps // 2), 0)
+
+    lax.fori_loop(0, 2 * side, outer, 0)
+
+
+def clear_factors(fact_y, fact_x):
+    def clear(i, _):
+        at = pl.ds(pl.multiple_of(i * 512, 512), 512)
+        fact_y[at, :] = jnp.zeros((512, 128), f32)
+        fact_x[at, :] = jnp.zeros((512, 128), f32)
+        return 0
+
+    lax.fori_loop(0, fact_y.shape[0] // 512, clear, 0)
 
 
 def lagrange(t):
@@ -250,14 +292,6 @@
     cell_col = iota((8, 128), 1) & 15
     sub = iota((8, 128), 0)
     zero = jnp.zeros((8, 128), f32)
-
-    def clear(i, _):
-        at = pl.ds(pl.multiple_of(i * 512, 512), 512)
-        fact_y[at, :] = jnp.zeros((512, 128), f32)
-        fact_x[at, :] = jnp.zeros((512, 128), f32)
-        return 0
-
-    lax.fori_loop(0, blocks // 64, clear, 0)
 
     def factors(i, _):
         for u in range(4):
@@ -283,8 +317,8 @@
             b = first + e
             lines = []
             for k in range(3):
-                d = (dep[k, b] + shift) & (total - 1)
-                lines.append(spread[pl.ds(pl.multiple_of(d * 32, 32), 32), :])
+                d = jnp.minimum((dep[k, b] + shift) & (total - 1), blocks + 2 * reach - 1)
+                lines.append(spread[d])
             uy = (sub + 1) - jnp.broadcast_to(floors[0, pl.ds(b, 1), :], (8, 128))
             ux = (sub + 1) - jnp.broadcast_to(floors[1, pl.ds(b, 1), :], (8, 128))
             at = pl.ds(pl.multiple_of(b * 8, 8), 8)
@@ -310,11 +344,7 @@
             out[pl.ds(pl.multiple_of(b * 4, 16), 16), :] = four
         return 0
 
-    lax.fori_loop(0, blocks // STEP, some, 0)
-
-
-def in_vmem(n):
-    return [pl.BlockSpec(memory_space=pltpu.VMEM)] * n
+    return some
 
 
 def on_device(tracers, winds, tile_owner, departure):
@@ -325,18 +355,16 @@
     lines = tracers.reshape(panel, blocks, 128).transpose(1, 0, 2).reshape(blocks * panel, 128)
     wind_lines = winds.reshape(2, blocks, 128).transpose(1, 0, 2).reshape(blocks * 2, 128)
     dma = pltpu.SemaphoreType.DMA
-    words, spread = pl.pallas_call(
-        exchange,
-        out_shape=(
-            jax.ShapeDtypeStruct((blocks, 128), i32),
-            jax.ShapeDtypeStruct((blocks * 48, 128), bf16),
-        ),
-        in_specs=[pl.BlockSpec(memory_space=pltpu.HBM)] * 3,
-        out_specs=tuple(in_vmem(2)),
+    out = pl.pallas_call(
+        advect,
+        out_shape=jax.ShapeDtypeStruct((blocks * panel, 128), bf16),
+        in_specs=[pl.BlockSpec(memory_space=pltpu.HBM)] * 4,
+        out_specs=pl.BlockSpec(memory_space=pltpu.VMEM),
         scratch_shapes=[
             pltpu.VMEM((blocks * 2, 128), f32),
             pltpu.VMEM((blocks // 128, 128), i32),
             pltpu.VMEM((blocks * panel, 128), bf16),
+            pltpu.SMEM((3, blocks), i32),
             pltpu.VMEM((edge, 128), bf16),
             pltpu.VMEM((edge, 128), bf16),
             pltpu.VMEM((blocks, 512), bf16),
@@ -344,30 +372,23 @@
             pltpu.VMEM((pieces, 8, 128), i32),
             pltpu.VMEM((4, blocks // 4 + 8, 128), i32),
             pltpu.VMEM((8, 128), i32),
+            pltpu.VMEM((blocks, 128), i32),
+            pltpu.VMEM((blocks * 3 // 2, 32, 128), bf16),
+            pltpu.VMEM((blocks * 8, 128), f32),
+            pltpu.VMEM((blocks * 8, 128), f32),
+            pltpu.VMEM((2, blocks, 128), i32),
             dma((pieces,)),
             dma((pieces,)),
             dma((2,)),
             dma((2,)),
+            dma((6,)),
+            dma((4, 2)),
             dma((4,)),
-            dma((4,)),
-            dma((3,)),
         ],
         compiler_params=pltpu.CompilerParams(
-            collective_id=0, has_side_effects=True, vmem_limit_bytes=36 << 20
+            collective_id=0, has_side_effects=True, vmem_limit_bytes=60 << 20
         ),
-    )(wind_lines, tile_owner.reshape(blocks // 128, 128), lines)
-    out = pl.pallas_call(
-        transport,
-        out_shape=jax.ShapeDtypeStruct((blocks * panel, 128), bf16),
-        in_specs=[pl.BlockSpec(memory_space=pltpu.SMEM)] + in_vmem(2),
-        out_specs=in_vmem(1)[0],
-        scratch_shapes=[
-            pltpu.VMEM((blocks * 8, 128), f32),
-            pltpu.VMEM((blocks * 8, 128), f32),
-            pltpu.VMEM((2, blocks, 128), i32),
-        ],
-        compiler_params=pltpu.CompilerParams(vmem_limit_bytes=36 << 20),
-    )(departure.T, words, spread)
+    )(wind_lines, tile_owner.reshape(blocks // 128, 128), lines, departure.T)
     return out.reshape(blocks, panel, 128).transpose(1, 0, 2).reshape(panel, blocks * 128)
 
 

time: 55.6 us -> 48.2 us (0.87)
  Pallas kernels: 51.5 us -> 45.5 us
  local copies, waits for them, and re-layouts: 3.85 us -> 2.56 us
    pallas_call x2 -> x1, Pallas kernels: 51.5 us -> 45.5 us  [on_device(): pl.pallas_call(advect, out_shape=jax.ShapeDtypeStruct((blocks * panel, 12...]
    unnamed x8 -> x1, local copies, waits for them, and re-layouts: 3.85 us -> 2.56 us
where the time goes in v2:
time: 48.2 us; the launch traced here: 48 us
  Pallas kernels  45.5 us (94%)
  local copies, waits for them, and re-layouts  2.56 us (5%)
    pallas_call x1, Pallas kernels, on_device(): pl.pallas_call(advect, out_shape=jax.ShapeDtypeStruct((blocks * panel, 12...  45.5 us
    unnamed x1, local copies, waits for them, and re-layouts  2.56 us

profile of v2, /device:TPU:1, one launch (start us, length us, event | category | flops | bytes accessed | tf_op | source)
XLA Modules:
  0.0 48.0 jit_solution(12733416102548470523)
XLA Ops:
  0.0 45.5 %shard_map.46 = bf16[4096,128]{1,0:T(8,128)(2,1)} custom-call(f32[2048,128]{1,0:T(8,128)} %bitcast.18, s32[8,128]{1,0:T(8,128)} %bitcast.21, bf16[4096,128]{1,0:T(8,128)(2,1)} %bitcast.19, s32[3,1024]{1,0:T(4,128)} %bitcast.20), custom_call_target="tpu_custom_call" | custom-call | tf_op jit(solution)/shard_map/pallas_call | solution.py:358
  45.5 2.6 %copy.9 = bf16[4,131072]{1,0:T(4,128)(2,1)} copy(bf16[4,131072]{1,0:T(4,128)(2,1)} %bitcast.17) | data formatting | bytes 2097152

commit v3 on v2

--- a/solution.py
+++ b/solution.py
@@ -134,10 +134,11 @@
         )
 
     def start(i, _):
-        message(lax.rem(me + i, pieces), me).start()
-        return 0
-
-    lax.fori_loop(1, pieces, start, 0)
+        ahead = 1 + lax.rem(i + pieces // 4, pieces - 1)
+        message(lax.rem(me + ahead, pieces), me).start()
+        return 0
+
+    lax.fori_loop(0, pieces - 1, start, 0)
 
     up = pltpu.make_async_remote_copy(
         src_ref=tracers_hbm.at[pl.ds(tracers.shape[0] - edge, edge)],
@@ -174,9 +175,7 @@
 
     def finish(i, _):
         other = lax.rem(me + i, pieces)
-        copy = message(other, other)
-        copy.wait_send()
-        copy.wait_recv()
+        message(other, other).wait_recv()
         return 0
 
     lax.fori_loop(1, pieces, finish, 0)
@@ -220,8 +219,6 @@
     handed(right, 0, right, 0).wait_recv()
     handed(far, 0, left, 0).wait_recv()
     handed(far, 1, right, 0).wait_recv()
-    for copy in sends:
-        copy.wait_send()
 
     for c in range(4):
         where[2 * c : 2 * c + 2, :] = every[c, share : share + 2, :]
@@ -232,13 +229,13 @@
             parts[at : at + 64, :] = jnp.concatenate(bytes_of(y) + bytes_of(x), 1)
 
     def settle(i, _):
-        base = i * share
-        words[pl.ds(pl.multiple_of(base, share), share), :] = joined(
-            jnp.dot(one_hot(base, share), parts[...], preferred_element_type=f32)
+        base = i * 512
+        words[pl.ds(pl.multiple_of(base, 512), 512), :] = joined(
+            jnp.dot(one_hot(base, 512), parts[...], preferred_element_type=f32)
         )
         return 0
 
-    lax.fori_loop(0, 4, settle, 0)
+    lax.fori_loop(0, 2, settle, 0)
     load_dep.wait()
     step_of = transport(dep, words, spread, out, fact_y, fact_x, floors)
     steps = blocks // STEP
@@ -254,6 +251,28 @@
         return step_of(i + (i // side) * (steps // 2), 0)
 
     lax.fori_loop(0, 2 * side, outer, 0)
+
+    def sent(i, _):
+        message(lax.rem(me + i, pieces), me).wait_send()
+        return 0
+
+    lax.fori_loop(1, pieces, sent, 0)
+    for copy in sends:
+        copy.wait_send()
+
+
+def hand_out(whole, out, sems):
+    piece = out.shape[0] // 4
+    copies = [
+        pltpu.make_async_copy(
+            whole.at[pl.ds(i * piece, piece)], out.at[pl.ds(i * piece, piece)], sems.at[i]
+        )
+        for i in range(4)
+    ]
+    for copy in copies:
+        copy.start()
+    for copy in copies:
+        copy.wait()
 
 
 def clear_factors(fact_y, fact_x):
@@ -389,6 +408,14 @@
             collective_id=0, has_side_effects=True, vmem_limit_bytes=60 << 20
         ),
     )(wind_lines, tile_owner.reshape(blocks // 128, 128), lines, departure.T)
+    out = pl.pallas_call(
+        hand_out,
+        out_shape=jax.ShapeDtypeStruct(out.shape, bf16),
+        in_specs=[pl.BlockSpec(memory_space=pltpu.HBM)],
+        out_specs=pl.BlockSpec(memory_space=pltpu.HBM),
+        scratch_shapes=[dma((4,))],
+        compiler_params=pltpu.CompilerParams(vmem_limit_bytes=60 << 20),
+    )(out)
     return out.reshape(blocks, panel, 128).transpose(1, 0, 2).reshape(panel, blocks * 128)
 
 

time: 48.2 us -> 79 us (1.64)
  Pallas kernels: 45.5 us -> 78.6 us
  local copies, waits for them, and re-layouts: 2.56 us -> 0 us
    pallas_call x0 -> x1, Pallas kernels: none -> 32.9 us  [on_device(): pl.pallas_call(hand_out, out_shape=jax.ShapeDtypeStruct(out.shape, bf16),...]
    unnamed x1 -> x0, local copies, waits for them, and re-layouts: 2.56 us -> none
where the time goes in v3:
time: 79 us; the launch traced here: 78.6 us
  Pallas kernels  78.6 us (99%)
    pallas_call x1, Pallas kernels, on_device(): pl.pallas_call(advect, out_shape=jax.ShapeDtypeStruct((blocks * panel, 12...  45.7 us
    pallas_call x1, Pallas kernels, on_device(): pl.pallas_call(hand_out, out_shape=jax.ShapeDtypeStruct(out.shape, bf16),...  32.9 us

profile of v3, /device:TPU:1, one launch (start us, length us, event | category | flops | bytes accessed | tf_op | source)
XLA Modules:
  0.0 78.6 jit_solution(1557611377186684730)
XLA Ops:
  0.0 45.7 %shard_map.46.whole = bf16[4096,128]{1,0:T(8,128)(2,1)} custom-call(f32[2048,128]{1,0:T(8,128)} %bitcast.17, s32[8,128]{1,0:T(8,128)} %bitcast.20, bf16[4096,128]{1,0:T(8,128)(2,1)} %bitcast.18, s32[3,1024]{1,0:T(4,128)} %bitcast.19), custom_call_target="tpu_custom_call" | custom-call | tf_op jit(solution)/shard_map/pallas_call | solution.py:377
  45.7 32.9 %shard_map.47 = bf16[4096,128]{1,0:T(8,128)(2,1)} custom-call(bf16[4096,128]{1,0:T(8,128)(2,1)} %shard_map.46.whole), custom_call_target="tpu_custom_call" | custom-call | tf_op jit(solution)/shard_map/pallas_call | solution.py:411

commit v4 on v3

--- a/solution.py
+++ b/solution.py
@@ -12,7 +12,7 @@
 MESH = pl.DeviceIdType.MESH
 ROWS = 5
 UNIT = 4096
-STEP = 64
+STEP = 128
 
 
 def iota(shape, dim):
@@ -40,7 +40,7 @@
 def advect(
     winds_hbm, owner_hbm, tracers_hbm, dep_hbm, out,
     winds, owner, tracers, dep, low, high, parts, snd, rcv, every, where,
-    words, spread, fact_y, fact_x, floors,
+    words, spread, fact_y, fact_x, floors, dep_far, dep_near, cells, out_sem,
     send_sem, recv_sem, halo_send, halo_recv, pass_send, pass_recv, load_sem,
 ):
     pieces = snd.shape[0]
@@ -70,7 +70,7 @@
     load_owner.start()
     load_winds.start()
     load_tracers.start()
-    load_dep = pltpu.make_async_copy(dep_hbm, dep, load_sem.at[3])
+    load_dep = pltpu.make_async_copy(dep_hbm, dep_far, load_sem.at[3])
     load_dep.start()
 
     load_owner.wait()
@@ -173,6 +173,15 @@
     widen(tracers, edge // 32)
     clear_factors(fact_y, fact_x)
 
+    load_dep.wait()
+    reach = blocks // 4
+    ahead = dep_far[...] - (me * blocks - reach)
+    total = blocks * pieces
+    ahead = jnp.where(ahead < 0, ahead + total, jnp.where(ahead >= total, ahead - total, ahead))
+    dep_near[...] = jnp.clip(ahead, 0, blocks + 2 * reach - 1)
+    place_dep = pltpu.make_async_copy(dep_near, dep, load_sem.at[4])
+    place_dep.start()
+
     def finish(i, _):
         other = lax.rem(me + i, pieces)
         message(other, other).wait_recv()
@@ -236,12 +245,19 @@
         return 0
 
     lax.fori_loop(0, 2, settle, 0)
-    load_dep.wait()
-    step_of = transport(dep, words, spread, out, fact_y, fact_x, floors)
+    place_dep.wait()
+    step_of = transport(dep, words, spread, cells, fact_y, fact_x, floors)
     steps = blocks // STEP
     side = steps // 4
 
     lax.fori_loop(side, steps - side, step_of, 0)
+    quarter = cells.shape[0] // 4
+
+    def leave(first, count, i):
+        at = pl.ds(first * quarter, count * quarter)
+        return pltpu.make_async_copy(cells.at[at], out.at[at], out_sem.at[i])
+
+    leave(1, 2, 0).start()
     up.wait()
     widen(low, 0)
     down.wait()
@@ -251,6 +267,8 @@
         return step_of(i + (i // side) * (steps // 2), 0)
 
     lax.fori_loop(0, 2 * side, outer, 0)
+    leave(0, 1, 1).start()
+    leave(3, 1, 2).start()
 
     def sent(i, _):
         message(lax.rem(me + i, pieces), me).wait_send()
@@ -259,19 +277,22 @@
     lax.fori_loop(1, pieces, sent, 0)
     for copy in sends:
         copy.wait_send()
-
-
-def hand_out(whole, out, sems):
+    leave(1, 2, 0).wait()
+    leave(0, 1, 1).wait()
+    leave(3, 1, 2).wait()
+
+
+def hand_out(whole, out, held, in_sem, out_sem):
     piece = out.shape[0] // 4
-    copies = [
-        pltpu.make_async_copy(
-            whole.at[pl.ds(i * piece, piece)], out.at[pl.ds(i * piece, piece)], sems.at[i]
-        )
-        for i in range(4)
-    ]
-    for copy in copies:
+    at = [pl.ds(i * piece, piece) for i in range(4)]
+    entering = [pltpu.make_async_copy(whole.at[p], held.at[p], in_sem.at[i]) for i, p in enumerate(at)]
+    leaving = [pltpu.make_async_copy(held.at[p], out.at[p], out_sem.at[i]) for i, p in enumerate(at)]
+    for copy in entering:
         copy.start()
-    for copy in copies:
+    for first, second in zip(entering, leaving):
+        first.wait()
+        second.start()
+    for copy in leaving:
         copy.wait()
 
 
@@ -304,9 +325,6 @@
 
 def transport(dep, words, spread, out, fact_y, fact_x, floors):
     blocks = words.shape[0]
-    reach = blocks // 4
-    total = blocks * lax.axis_size(AXES)
-    shift = reach - lax.axis_index(AXES) * blocks + total
     cell_row = iota((8, 128), 1) >> 4
     cell_col = iota((8, 128), 1) & 15
     sub = iota((8, 128), 0)
@@ -336,8 +354,7 @@
             b = first + e
             lines = []
             for k in range(3):
-                d = jnp.minimum((dep[k, b] + shift) & (total - 1), blocks + 2 * reach - 1)
-                lines.append(spread[d])
+                lines.append(spread[dep[k, b]])
             uy = (sub + 1) - jnp.broadcast_to(floors[0, pl.ds(b, 1), :], (8, 128))
             ux = (sub + 1) - jnp.broadcast_to(floors[1, pl.ds(b, 1), :], (8, 128))
             at = pl.ds(pl.multiple_of(b * 8, 8), 8)
@@ -378,7 +395,7 @@
         advect,
         out_shape=jax.ShapeDtypeStruct((blocks * panel, 128), bf16),
         in_specs=[pl.BlockSpec(memory_space=pltpu.HBM)] * 4,
-        out_specs=pl.BlockSpec(memory_space=pltpu.VMEM),
+        out_specs=pl.BlockSpec(memory_space=pltpu.HBM),
         scratch_shapes=[
             pltpu.VMEM((blocks * 2, 128), f32),
             pltpu.VMEM((blocks // 128, 128), i32),
@@ -396,13 +413,17 @@
             pltpu.VMEM((blocks * 8, 128), f32),
             pltpu.VMEM((blocks * 8, 128), f32),
             pltpu.VMEM((2, blocks, 128), i32),
+            pltpu.VMEM((3, blocks), i32),
+            pltpu.VMEM((3, blocks), i32),
+            pltpu.VMEM((blocks * panel, 128), bf16),
+            dma((3,)),
             dma((pieces,)),
             dma((pieces,)),
             dma((2,)),
             dma((2,)),
             dma((6,)),
             dma((4, 2)),
-            dma((4,)),
+            dma((5,)),
         ],
         compiler_params=pltpu.CompilerParams(
             collective_id=0, has_side_effects=True, vmem_limit_bytes=60 << 20
@@ -413,7 +434,7 @@
         out_shape=jax.ShapeDtypeStruct(out.shape, bf16),
         in_specs=[pl.BlockSpec(memory_space=pltpu.HBM)],
         out_specs=pl.BlockSpec(memory_space=pltpu.HBM),
-        scratch_shapes=[dma((4,))],
+        scratch_shapes=[pltpu.VMEM(out.shape, bf16), dma((4,)), dma((4,))],
         compiler_params=pltpu.CompilerParams(vmem_limit_bytes=60 << 20),
     )(out)
     return out.reshape(blocks, panel, 128).transpose(1, 0, 2).reshape(panel, blocks * 128)

time: 79 us -> 44.9 us (0.57)
  Pallas kernels: 78.6 us -> 44.5 us
    pallas_call x1, Pallas kernels: 32.9 us -> 1.98 us  [on_device(): pl.pallas_call(hand_out, out_shape=jax.ShapeDtypeStruct(out.shape, bf16),...]
    pallas_call x1, Pallas kernels: 45.7 us -> 42.5 us  [on_device(): pl.pallas_call(advect, out_shape=jax.ShapeDtypeStruct((blocks * panel, 12...]
where the time goes in v4:
time: 44.9 us; the launch traced here: 44.5 us
  Pallas kernels  44.5 us (99%)
    pallas_call x1, Pallas kernels, on_device(): pl.pallas_call(advect, out_shape=jax.ShapeDtypeStruct((blocks * panel, 12...  42.5 us
    pallas_call x1, Pallas kernels, on_device(): pl.pallas_call(hand_out, out_shape=jax.ShapeDtypeStruct(out.shape, bf16),...  1.98 us

profile of v4, /device:TPU:1, one launch (start us, length us, event | category | flops | bytes accessed | tf_op | source)
XLA Modules:
  0.0 44.5 jit_solution(1415037782488674377)
XLA Ops:
  0.0 42.5 %shard_map.46.whole = bf16[4096,128]{1,0:T(8,128)(2,1)} custom-call(f32[2048,128]{1,0:T(8,128)} %bitcast.17, s32[8,128]{1,0:T(8,128)} %bitcast.20, bf16[4096,128]{1,0:T(8,128)(2,1)} %bitcast.18, s32[3,1024]{1,0:T(4,128)} %bitcast.19), custom_call_target="tpu_custom_call" | custom-call | tf_op jit(solution)/shard_map/pallas_call | solution.py:394
  42.5 2.0 %shard_map.47 = bf16[4096,128]{1,0:T(8,128)(2,1)} custom-call(bf16[4096,128]{1,0:T(8,128)(2,1)} %shard_map.46.whole), custom_call_target="tpu_custom_call" | custom-call | tf_op jit(solution)/shard_map/pallas_call | solution.py:432

commit v5 on v4

--- a/solution.py
+++ b/solution.py
@@ -78,7 +78,6 @@
     step = jnp.concatenate([pick(iota((128, 128), 0) < lanes), jnp.ones((128, 128), bf16)], 1)
     run = jnp.zeros((pieces, 128), f32)
     sums = jnp.zeros((pieces, 128), f32)
-    first_lane = lax.rem(me, 32) * 4
     for g in range(blocks // 128):
         own = owner[g : g + 1, :]
         to = own // blocks
@@ -91,7 +90,9 @@
         run = run + seen[:, 128:]
         here = (rank >= 0) & (rank < 4)
         where[g : g + 1, :] = jnp.where(here, to * 4 + rank, -1)
-        lane = iota((128, 128), 0) == jnp.where(here, rank + first_lane, -1)
+        turn = to - me + (pieces - 1)
+        turn = jnp.where(turn >= pieces, turn - pieces, turn)
+        lane = iota((128, 128), 0) == jnp.where(here, rank + 4 * (turn & 31), -1)
         for part, scale in ((slot >> 5, 32.0), (slot & 31, 1.0)):
             spot = jnp.where(lane, part.astype(f32), 0.0).astype(bf16)
             sums = sums + scale * lax.dot_general(
@@ -123,19 +124,19 @@
 
     pl.semaphore_wait(barrier, pieces + 1)
 
-    def message(to, frm):
+    def message(turn):
+        to = lax.rem(me + turn + 1, pieces)
         return pltpu.make_async_remote_copy(
             src_ref=snd.at[to, pl.ds(0, ROWS)],
-            dst_ref=rcv.at[frm, pl.ds(0, ROWS)],
-            send_sem=send_sem.at[to],
-            recv_sem=recv_sem.at[frm],
+            dst_ref=rcv.at[turn, pl.ds(0, ROWS)],
+            send_sem=send_sem.at[turn],
+            recv_sem=recv_sem.at[turn],
             device_id=place_of(to),
             device_id_type=MESH,
         )
 
-    def start(i, _):
-        ahead = 1 + lax.rem(i + pieces // 4, pieces - 1)
-        message(lax.rem(me + ahead, pieces), me).start()
+    def start(turn, _):
+        message(turn).start()
         return 0
 
     lax.fori_loop(0, pieces - 1, start, 0)
@@ -156,7 +157,7 @@
         device_id=place_of(before),
         device_id_type=MESH,
     )
-    rcv[me, 0:ROWS, :] = snd[me, 0:ROWS, :]
+    rcv[pieces - 1, 0:ROWS, :] = snd[me, 0:ROWS, :]
 
     own_row = (iota((8, 128), 1) >> 4) == iota((8, 128), 0)
 
@@ -182,60 +183,66 @@
     place_dep = pltpu.make_async_copy(dep_near, dep, load_sem.at[4])
     place_dep.start()
 
-    def finish(i, _):
-        other = lax.rem(me + i, pieces)
-        message(other, other).wait_recv()
-        return 0
-
-    lax.fori_loop(1, pieces, finish, 0)
-
-    every[col, 0:share, :] = rcv[:, 0:4, :].reshape(share, 128)
-    for h in range(2):
-        rows = [rcv[32 * h + s, 4:5, :] for s in range(32)]
-        every[col, share + h : share + h + 1, :] = functools.reduce(jnp.add, rows)
-
-    cut = (share + 8) // 16 * 8 + 8
+    def arrive(turn, _):
+        message(turn).wait_recv()
+        return 0
+
+    far = lax.rem(col + 2, 4)
+
+    def gather(half):
+        at = pl.ds(32 * half, 32)
+        every[col, half, 0:128, :] = rcv[at, 0:4, :].reshape(128, 128)
+        rows = [rcv[32 * half + s, 4:5, :] for s in range(32)]
+        every[col, half, 128:129, :] = functools.reduce(jnp.add, rows)
 
     def handed(origin, half, to, send):
-        at = pl.ds(0, cut) if half == 0 else pl.ds(cut, share + 8 - cut)
         return pltpu.make_async_remote_copy(
-            src_ref=every.at[origin, at],
-            dst_ref=every.at[origin, at],
+            src_ref=every.at[origin, half],
+            dst_ref=every.at[origin, half],
             send_sem=pass_send.at[send],
             recv_sem=pass_recv.at[origin, half],
             device_id={"col": to},
             device_id_type=MESH,
         )
 
-    far = lax.rem(col + 2, 4)
-    sends = [
-        handed(col, 0, right, 0),
-        handed(col, 1, left, 1),
-        handed(col, 1, right, 2),
-        handed(col, 0, left, 3),
-    ]
-    for copy in sends:
-        copy.start()
+    def unpack(origin, half):
+        where[pl.ds(2 * origin + half, 1), :] = every[origin, half, 128:129, :]
+        for i in range(2):
+            word = every[origin, half, 64 * i : 64 * i + 64, :]
+            y, x = word >> 16, (word << 16) >> 16
+            at = pl.ds(pl.multiple_of(origin * share + half * 128 + 64 * i, 64), 64)
+            parts[at, :] = jnp.concatenate(bytes_of(y) + bytes_of(x), 1)
+
+    lax.fori_loop(0, 32, arrive, 0)
+    gather(0)
+    sends = [handed(col, 0, right, 0), handed(col, 0, left, 1)]
+    sends[0].start()
+    sends[1].start()
+    unpack(col, 0)
+    handed(left, 0, left, 0).wait_recv()
+    sends.append(handed(left, 0, right, 2))
+    sends[2].start()
+    unpack(left, 0)
+    lax.fori_loop(32, pieces - 1, arrive, 0)
+    gather(1)
+    sends += [handed(col, 1, left, 3), handed(col, 1, right, 4)]
+    sends[3].start()
+    sends[4].start()
     up.start()
     down.start()
-    handed(left, 0, left, 0).wait_recv()
-    sends.append(handed(left, 0, right, 4))
-    sends[-1].start()
+    unpack(col, 1)
+    handed(right, 0, right, 0).wait_recv()
+    unpack(right, 0)
     handed(right, 1, right, 0).wait_recv()
     sends.append(handed(right, 1, left, 5))
-    sends[-1].start()
+    sends[5].start()
+    unpack(right, 1)
     handed(left, 1, left, 0).wait_recv()
-    handed(right, 0, right, 0).wait_recv()
+    unpack(left, 1)
     handed(far, 0, left, 0).wait_recv()
+    unpack(far, 0)
     handed(far, 1, right, 0).wait_recv()
-
-    for c in range(4):
-        where[2 * c : 2 * c + 2, :] = every[c, share : share + 2, :]
-        for i in range(4):
-            word = every[c, 64 * i : 64 * i + 64, :]
-            y, x = word >> 16, (word << 16) >> 16
-            at = c * share + 64 * i
-            parts[at : at + 64, :] = jnp.concatenate(bytes_of(y) + bytes_of(x), 1)
+    unpack(far, 1)
 
     def settle(i, _):
         base = i * 512
@@ -270,11 +277,11 @@
     leave(0, 1, 1).start()
     leave(3, 1, 2).start()
 
-    def sent(i, _):
-        message(lax.rem(me + i, pieces), me).wait_send()
-        return 0
-
-    lax.fori_loop(1, pieces, sent, 0)
+    def sent(turn, _):
+        message(turn).wait_send()
+        return 0
+
+    lax.fori_loop(0, pieces - 1, sent, 0)
     for copy in sends:
         copy.wait_send()
     leave(1, 2, 0).wait()
@@ -406,7 +413,7 @@
             pltpu.VMEM((blocks, 512), bf16),
             pltpu.VMEM((pieces, 8, 128), i32),
             pltpu.VMEM((pieces, 8, 128), i32),
-            pltpu.VMEM((4, blocks // 4 + 8, 128), i32),
+            pltpu.VMEM((4, 2, 136, 128), i32),
             pltpu.VMEM((8, 128), i32),
             pltpu.VMEM((blocks, 128), i32),
             pltpu.VMEM((blocks * 3 // 2, 32, 128), bf16),

time: 44.9 us -> 47.9 us (1.067)
  the two profiles are of different devices: /device:TPU:1 before, /device:TPU:4 now
where the time goes in v5:
time: 47.9 us; the launch traced here: 47.8 us
  Pallas kernels  47.8 us (100%)
    pallas_call x1, Pallas kernels, on_device(): pl.pallas_call(advect, out_shape=jax.ShapeDtypeStruct((blocks * panel, 12...  45.8 us
    pallas_call x1, Pallas kernels, on_device(): pl.pallas_call(hand_out, out_shape=jax.ShapeDtypeStruct(out.shape, bf16),...  1.98 us

profile of v5, /device:TPU:4, one launch (start us, length us, event | category | flops | bytes accessed | tf_op | source)
XLA Modules:
  0.0 47.8 jit_solution(1126436955442581595)
XLA Ops:
  0.0 45.8 %shard_map.46.whole = bf16[4096,128]{1,0:T(8,128)(2,1)} custom-call(f32[2048,128]{1,0:T(8,128)} %bitcast.17, s32[8,128]{1,0:T(8,128)} %bitcast.20, bf16[4096,128]{1,0:T(8,128)(2,1)} %bitcast.18, s32[3,1024]{1,0:T(4,128)} %bitcast.19), custom_call_target="tpu_custom_call" | custom-call | tf_op jit(solution)/shard_map/pallas_call | solution.py:401
  45.8 2.0 %shard_map.47 = bf16[4096,128]{1,0:T(8,128)(2,1)} custom-call(bf16[4096,128]{1,0:T(8,128)(2,1)} %shard_map.46.whole), custom_call_target="tpu_custom_call" | custom-call | tf_op jit(solution)/shard_map/pallas_call | solution.py:439

commit v6 on v5

--- a/solution.py
+++ b/solution.py
@@ -90,8 +90,10 @@
         run = run + seen[:, 128:]
         here = (rank >= 0) & (rank < 4)
         where[g : g + 1, :] = jnp.where(here, to * 4 + rank, -1)
-        turn = to - me + (pieces - 1)
-        turn = jnp.where(turn >= pieces, turn - pieces, turn)
+        ahead = jnp.where(to >= me, to - me, to - me + pieces)
+        turn = ahead - 1 - pieces // 4
+        turn = jnp.where(turn < 0, turn + pieces - 1, turn)
+        turn = jnp.where(ahead == 0, pieces - 1, turn)
         lane = iota((128, 128), 0) == jnp.where(here, rank + 4 * (turn & 31), -1)
         for part, scale in ((slot >> 5, 32.0), (slot & 31, 1.0)):
             spot = jnp.where(lane, part.astype(f32), 0.0).astype(bf16)
@@ -125,7 +127,7 @@
     pl.semaphore_wait(barrier, pieces + 1)
 
     def message(turn):
-        to = lax.rem(me + turn + 1, pieces)
+        to = lax.rem(me + 1 + lax.rem(turn + pieces // 4, pieces - 1), pieces)
         return pltpu.make_async_remote_copy(
             src_ref=snd.at[to, pl.ds(0, ROWS)],
             dst_ref=rcv.at[turn, pl.ds(0, ROWS)],
@@ -219,18 +221,18 @@
     sends[0].start()
     sends[1].start()
     unpack(col, 0)
-    handed(left, 0, left, 0).wait_recv()
-    sends.append(handed(left, 0, right, 2))
-    sends[2].start()
-    unpack(left, 0)
     lax.fori_loop(32, pieces - 1, arrive, 0)
     gather(1)
-    sends += [handed(col, 1, left, 3), handed(col, 1, right, 4)]
+    sends += [handed(col, 1, left, 2), handed(col, 1, right, 3)]
+    sends[2].start()
     sends[3].start()
-    sends[4].start()
     up.start()
     down.start()
+    handed(left, 0, left, 0).wait_recv()
+    sends.append(handed(left, 0, right, 4))
+    sends[4].start()
     unpack(col, 1)
+    unpack(left, 0)
     handed(right, 0, right, 0).wait_recv()
     unpack(right, 0)
     handed(right, 1, right, 0).wait_recv()

time: 47.9 us -> 44.2 us (0.923)
  the two profiles are of different devices: /device:TPU:4 before, /device:TPU:1 now
where the time goes in v6:
time: 44.2 us; the launch traced here: 44.1 us
  Pallas kernels  44.1 us (100%)
    pallas_call x1, Pallas kernels, on_device(): pl.pallas_call(advect, out_shape=jax.ShapeDtypeStruct((blocks * panel, 12...  42.1 us
    pallas_call x1, Pallas kernels, on_device(): pl.pallas_call(hand_out, out_shape=jax.ShapeDtypeStruct(out.shape, bf16),...  1.98 us

profile of v6, /device:TPU:1, one launch (start us, length us, event | category | flops | bytes accessed | tf_op | source)
XLA Modules:
  0.0 44.1 jit_solution(14087918589946597177)
XLA Ops:
  0.0 42.1 %shard_map.46.whole = bf16[4096,128]{1,0:T(8,128)(2,1)} custom-call(f32[2048,128]{1,0:T(8,128)} %bitcast.17, s32[8,128]{1,0:T(8,128)} %bitcast.20, bf16[4096,128]{1,0:T(8,128)(2,1)} %bitcast.18, s32[3,1024]{1,0:T(4,128)} %bitcast.19), custom_call_target="tpu_custom_call" | custom-call | tf_op jit(solution)/shard_map/pallas_call | solution.py:403
  42.1 2.0 %shard_map.47 = bf16[4096,128]{1,0:T(8,128)(2,1)} custom-call(bf16[4096,128]{1,0:T(8,128)(2,1)} %shard_map.46.whole), custom_call_target="tpu_custom_call" | custom-call | tf_op jit(solution)/shard_map/pallas_call | solution.py:441

commit v7 on v6

--- a/solution.py
+++ b/solution.py
@@ -12,7 +12,7 @@
 MESH = pl.DeviceIdType.MESH
 ROWS = 5
 UNIT = 4096
-STEP = 128
+STEP = 256
 
 
 def iota(shape, dim):
@@ -256,26 +256,24 @@
     lax.fori_loop(0, 2, settle, 0)
     place_dep.wait()
     step_of = transport(dep, words, spread, cells, fact_y, fact_x, floors)
-    steps = blocks // STEP
-    side = steps // 4
-
-    lax.fori_loop(side, steps - side, step_of, 0)
     quarter = cells.shape[0] // 4
 
     def leave(first, count, i):
         at = pl.ds(first * quarter, count * quarter)
         return pltpu.make_async_copy(cells.at[at], out.at[at], out_sem.at[i])
 
-    leave(1, 2, 0).start()
-    up.wait()
-    widen(low, 0)
-    down.wait()
-    widen(high, (edge + tracers.shape[0]) // 32)
-
-    def outer(i, _):
-        return step_of(i + (i // side) * (steps // 2), 0)
-
-    lax.fori_loop(0, 2 * side, outer, 0)
+    def quarters(i, _):
+        @pl.when(i == 2)
+        def _():
+            leave(1, 2, 0).start()
+            up.wait()
+            widen(low, 0)
+            down.wait()
+            widen(high, (edge + tracers.shape[0]) // 32)
+
+        return step_of(lax.rem(i + 1, 3) + 2 * (i // 3), 0)
+
+    lax.fori_loop(0, blocks // STEP, quarters, 0)
     leave(0, 1, 1).start()
     leave(3, 1, 2).start()
 

time: 44.2 us -> 43.9 us (level)
  no operation moved by 1% of the time
where the time goes in v7:
time: 43.9 us; the launch traced here: 43.8 us
  Pallas kernels  43.8 us (100%)
    pallas_call x1, Pallas kernels, on_device(): pl.pallas_call(advect, out_shape=jax.ShapeDtypeStruct((blocks * panel, 12...  41.8 us
    pallas_call x1, Pallas kernels, on_device(): pl.pallas_call(hand_out, out_shape=jax.ShapeDtypeStruct(out.shape, bf16),...  1.98 us

profile of v7, /device:TPU:1, one launch (start us, length us, event | category | flops | bytes accessed | tf_op | source)
XLA Modules:
  0.0 43.8 jit_solution(14009632132411480387)
XLA Ops:
  0.0 41.8 %shard_map.46.whole = bf16[4096,128]{1,0:T(8,128)(2,1)} custom-call(f32[2048,128]{1,0:T(8,128)} %bitcast.17, s32[8,128]{1,0:T(8,128)} %bitcast.20, bf16[4096,128]{1,0:T(8,128)(2,1)} %bitcast.18, s32[3,1024]{1,0:T(4,128)} %bitcast.19), custom_call_target="tpu_custom_call" | custom-call | tf_op jit(solution)/shard_map/pallas_call | solution.py:401
  41.8 2.0 %shard_map.47 = bf16[4096,128]{1,0:T(8,128)(2,1)} custom-call(bf16[4096,128]{1,0:T(8,128)(2,1)} %shard_map.46.whole), custom_call_target="tpu_custom_call" | custom-call | tf_op jit(solution)/shard_map/pallas_call | solution.py:439

commit v8 on v7

--- a/solution.py
+++ b/solution.py
@@ -91,9 +91,7 @@
         here = (rank >= 0) & (rank < 4)
         where[g : g + 1, :] = jnp.where(here, to * 4 + rank, -1)
         ahead = jnp.where(to >= me, to - me, to - me + pieces)
-        turn = ahead - 1 - pieces // 4
-        turn = jnp.where(turn < 0, turn + pieces - 1, turn)
-        turn = jnp.where(ahead == 0, pieces - 1, turn)
+        turn = jnp.where(ahead >= pieces // 2, 2 * ahead - pieces, pieces - 1 - 2 * ahead)
         lane = iota((128, 128), 0) == jnp.where(here, rank + 4 * (turn & 31), -1)
         for part, scale in ((slot >> 5, 32.0), (slot & 31, 1.0)):
             spot = jnp.where(lane, part.astype(f32), 0.0).astype(bf16)
@@ -127,7 +125,8 @@
     pl.semaphore_wait(barrier, pieces + 1)
 
     def message(turn):
-        to = lax.rem(me + 1 + lax.rem(turn + pieces // 4, pieces - 1), pieces)
+        half = (turn + 1) // 2
+        to = lax.rem(me + pieces // 2 + half - 2 * half * lax.rem(turn, 2), pieces)
         return pltpu.make_async_remote_copy(
             src_ref=snd.at[to, pl.ds(0, ROWS)],
             dst_ref=rcv.at[turn, pl.ds(0, ROWS)],

time: 43.9 us -> 44.7 us (1.018)
  Pallas kernels: 43.8 us -> 44.6 us
    pallas_call x1, Pallas kernels: 41.8 us -> 42.6 us  [on_device(): pl.pallas_call(advect, out_shape=jax.ShapeDtypeStruct((blocks * panel, 12...]
where the time goes in v8:
time: 44.7 us; the launch traced here: 44.6 us
  Pallas kernels  44.6 us (100%)
    pallas_call x1, Pallas kernels, on_device(): pl.pallas_call(advect, out_shape=jax.ShapeDtypeStruct((blocks * panel, 12...  42.6 us
    pallas_call x1, Pallas kernels, on_device(): pl.pallas_call(hand_out, out_shape=jax.ShapeDtypeStruct(out.shape, bf16),...  1.98 us

profile of v8, /device:TPU:1, one launch (start us, length us, event | category | flops | bytes accessed | tf_op | source)
XLA Modules:
  0.0 44.6 jit_solution(4586121364981156588)
XLA Ops:
  0.0 42.6 %shard_map.46.whole = bf16[4096,128]{1,0:T(8,128)(2,1)} custom-call(f32[2048,128]{1,0:T(8,128)} %bitcast.17, s32[8,128]{1,0:T(8,128)} %bitcast.20, bf16[4096,128]{1,0:T(8,128)(2,1)} %bitcast.18, s32[3,1024]{1,0:T(4,128)} %bitcast.19), custom_call_target="tpu_custom_call" | custom-call | tf_op jit(solution)/shard_map/pallas_call | solution.py:400
  42.6 2.0 %shard_map.47 = bf16[4096,128]{1,0:T(8,128)(2,1)} custom-call(bf16[4096,128]{1,0:T(8,128)(2,1)} %shard_map.46.whole), custom_call_target="tpu_custom_call" | custom-call | tf_op jit(solution)/shard_map/pallas_call | solution.py:438
